TPU v7x, 32 devices: a whole 2x2x4 slice. The times are simulated.
32 devices in a mesh: ctx: 4 (over z), row: 2 (over y), col: 4 (over x, core).
Axes of the slice: x: 2, y: 2, z: 4, core: 2. Of those that a mesh axis runs over, the one named last changes fastest.
Arguments:
- tokens: bfloat16 [2048, 8192], P(('ctx', 'row'), 'col'), may hold values from -9 to 9
- w_query: bfloat16 [8192, 2048], P('ctx', 'col'), may hold values from -0.0625 to 0.0625
- key_value_weight: bfloat16 [8192, 512], P('ctx', 'col'), may hold values from -0.0625 to 0.0625
- segment: int32 [2048], P(('ctx', 'row')), may hold values from 0 to 7, never falling along the last dimension, each value on 1 to 1024 neighbouring positions
Outputs:
- attended: bfloat16 [2048, 2048], P(('ctx', 'row'), 'col')
Inputs may be any that keep to these rules, and one draw needn't show every extreme that they name: `segment`: document ids never fall along the sequence; a document holds 1 to 1024 tokens.
All inputs are finite; a program needn't handle non-finite values.
Results may differ from a plain program's by a relative error of at most 0.011.
Values may be sent and summed in bfloat16 or wider, within the bound.
A program may use at most 64 MiB of HBM per device.

v0:
```python
import math
import jax
import jax.numpy as jnp
from jax import lax
from jax.sharding import PartitionSpec as P


def swapped(x, axis, stride):
    return lax.ppermute(x, axis, [(i, i ^ 1 << stride) for i in range(lax.axis_size(axis))])


def passed_along(x, axis, by):
    peers = lax.axis_size(axis)
    pairs = [(i, i + by) for i in range(peers) if 0 <= i + by < peers]
    return lax.ppermute(x, axis, pairs)


def local(tokens, w_query, key_value_weight, segment):
    half = tokens.shape[0]
    head_size = key_value_weight.shape[1]
    whole = lax.all_gather(tokens, "col", axis=1, tiled=True)
    query_acc = jnp.dot(
        whole,
        lax.all_gather(w_query, "ctx", axis=0, tiled=True),
        preferred_element_type=jnp.float32,
    )
    keyval_acc = jnp.dot(
        whole,
        lax.all_gather(key_value_weight, "ctx", axis=0, tiled=True),
        preferred_element_type=jnp.float32,
    )
    query = query_acc.astype(jnp.bfloat16)
    mine = keyval_acc.astype(jnp.bfloat16)
    is_even = lax.axis_index("col") % 2 == 0
    partner = swapped(mine, "col", 0)
    joined = jnp.concatenate(
        [jnp.where(is_even, mine, partner), jnp.where(is_even, partner, mine)], axis=1
    )
    block_kv, block_seg = (
        lax.all_gather(joined, "row", axis=0, tiled=True),
        lax.all_gather(segment, "row", axis=0, tiled=True),
    )
    prev_kv, prev_seg = passed_along((block_kv, block_seg), "ctx", 1)
    heads = query.shape[1] // head_size
    queries = query.reshape(half, heads, head_size)
    block = block_kv.shape[0]
    ctx_index = lax.axis_index("ctx")
    query_pos = lax.axis_index("row") * half + jnp.arange(half)
    key_pos = jnp.arange(block)
    own_allow = (key_pos[None, :] <= query_pos[:, None]) & (segment[:, None] == block_seg[None, :])
    prev_allow = (ctx_index > 0) & (segment[:, None] == prev_seg[None, :])
    scale = 1.0 / math.sqrt(head_size)

    def scores(key_value_rows, allow):
        score = (
            jnp.einsum(
                "qhd,kd->hqk",
                queries,
                key_value_rows[:, :head_size],
                preferred_element_type=jnp.float32,
            )
            * scale
        )
        return jnp.where(allow[None], score, -jnp.inf)

    parts = [(scores(block_kv, own_allow), block_kv), (scores(prev_kv, prev_allow), prev_kv)]
    top = parts[0][0].max(axis=-1, keepdims=True)
    for score, key_value_rows in parts[1:]:
        top = jnp.maximum(top, score.max(axis=-1, keepdims=True))
    total = jnp.zeros(top.shape[:2], jnp.float32)
    numer = jnp.zeros((half, heads, head_size), jnp.float32)
    for score, key_value_rows in parts:
        weight = jnp.exp(score - top)
        total = total + jnp.sum(weight, axis=-1)
        probs = weight.astype(jnp.bfloat16)
        numer = numer + jnp.einsum(
            "hqk,kd->qhd", probs, key_value_rows[:, head_size:], preferred_element_type=jnp.float32
        )
    result = (numer / jnp.transpose(total)[:, :, None]).astype(jnp.bfloat16)
    return result.reshape(half, heads * head_size)


def solution(mesh):
    in_specs = (P(("ctx", "row"), "col"), P("ctx", "col"), P("ctx", "col"), P(("ctx", "row")))
    out_specs = P(("ctx", "row"), "col")
    return jax.shard_map(local, mesh=mesh, in_specs=in_specs, out_specs=out_specs, check_vma=False)
```

profile of v0, /device:TPU:0, one launch (start us, length us, event | category | flops | bytes accessed | tf_op | source)
XLA Modules:
  0.0 262.4 jit_solution(787395383971608503)
XLA Ops:
  6.5 0.7 all-gather.7.cloned.1.call-update
  7.3 0.0 all-gather.5.cloned.1.call-start
  7.3 0.7 all-gather.5.cloned.1.call-update
  8.0 0.0 all-gather.9.cloned.1.call-start
  8.1 0.7 all-gather.9.cloned.1.call-update
  8.8 5.2 %all-gather = s32[2,1,256]{2,1,0:T(1,128)S(1)} all-gather(s32[1,1,256]{2,1,0:T(1,128)S(1)} %bitcast.56), channel_id=1, replica_groups=mesh['ctx'=4,'row'=2,'col'=4] {'row'}, dimensions={0}, use_global_device_ids=true | all-gather | bytes 3072 | tf_op jit(solution)/shard_map/all_gather | solution.py:41
  13.9 4.0 %collective-permute-start.1 = (s32[512]{0:T(512)S(1)}, s32[512]{0:T(512)S(1)}, u32[]{:S(2)}, u32[]{:S(2)}) collective-permute-start(s32[512]{0:T(512)S(1)} %bitcast.54), channel_id=1, source_target_pairs={{0,8},{8,16},{16,24},{1,9},{9,17},{17,25},{2,10},{10,18},{18,26},{... | collective-permute-start | bytes 6152 | tf_op jit(solution)/shard_map/ppermute | solution.py:15
  18.0 39.6 %all-gather.7.cloned.1.call-done = bf16[8192,128]{1,0:T(8,128)(2,1)} async-done(((bf16[2048,128]{1,0:T(8,128)(2,1)}), bf16[8192,128]{1,0:T(8,128)(2,1)}) %all-gather.7.cloned.1.call-update) | async-done | bytes 2097168 | tf_op jit(solution)/shard_map/all_gather | solution.py:29
  57.6 34.8 %all-gather.5.cloned.1.call-done = bf16[256,8192]{1,0:T(8,128)(2,1)} async-done(((bf16[256,2048]{1,0:T(8,128)(2,1)}), bf16[256,8192]{1,0:T(8,128)(2,1)}) %all-gather.5.cloned.1.call-update) | async-done | bytes 4194320 | tf_op jit(solution)/shard_map/all_gather | solution.py:21
  92.4 4.4 %convolution_convert_fusion.1 = bf16[256,128]{0,1:T(8,128)(2,1)S(1)} fusion(bf16[256,8192]{1,0:T(8,128)(2,1)} %all-gather.5.cloned.1.call-done, bf16[8192,128]{1,0:T(8,128)(2,1)} %all-gather.7.cloned.1.call-done), kind=kOutput, calls=%fused_computation.15 | convolution fusion | flops 536903680 | bytes 6356992 | tf_op jit(solution)/shard_map/dot_general | solution.py:27
  96.8 0.3 collective-permute-start
  97.1 0.0 collective-permute-done.1
  97.1 0.3 compare_and_fusion
  97.4 0.7 collective-permute-done
  98.1 6.3 %all_gather.17 = bf16[512,256]{0,1:T(8,128)(2,1)S(1)} all-gather(bf16[256,256]{0,1:T(8,128)(2,1)S(1)} %pad_maximum_fusion), channel_id=1, replica_groups=mesh['ctx'=4,'row'=2,'col'=4] {'row'}, dimensions={0}, use_global_device_ids=true | all-gather | bytes 393216 | tf_op jit(solution)/shard_map/all_gather | solution.py:40
  104.5 3.4 %collective-permute-start.2 = (bf16[512,256]{0,1:T(8,128)(2,1)S(1)}, bf16[512,256]{0,1:T(8,128)(2,1)S(1)}, u32[]{:S(2)}, u32[]{:S(2)}) collective-permute-start(bf16[512,256]{0,1:T(8,128)(2,1)S(1)} %all_gather.17), channel_id=1, source_target_pairs={{0,8},{8,16},{16,24},{1,9},{9,17},{17,25},{2,10},{10,18},{18,26},{... | collective-permute-start | bytes 786440 | tf_op jit(solution)/shard_map/ppermute | solution.py:15
  107.9 137.2 %all-gather.9.cloned.1.call-done = bf16[8192,512]{1,0:T(8,128)(2,1)} async-done(((bf16[2048,512]{1,0:T(8,128)(2,1)}), bf16[8192,512]{1,0:T(8,128)(2,1)}) %all-gather.9.cloned.1.call-update) | async-done | bytes 8388624 | tf_op jit(solution)/shard_map/all_gather | solution.py:24
  245.1 7.0 %fusion.8 = bf16[32,4,8,128]{3,2,1,0:T(8,128)(2,1)S(1)} fusion(bf16[256,8192]{1,0:T(8,128)(2,1)} %all-gather.5.cloned.1.call-done, bf16[8192,512]{1,0:T(8,128)(2,1)} %all-gather.9.cloned.1.call-done), kind=kOutput, calls=%fused_computation.14 | convolution fusion | flops 2147614720 | bytes 12845056 | tf_op jit(solution)/shard_map/dot_general | solution.py:22
  252.1 0.5 fusion.25
  252.6 0.5 fusion.4
  253.1 0.5 fusion.10
  253.6 0.7 fusion.2
  254.3 0.7 fusion.7
  255.0 0.8 copy.18
  (9 shorter events, 0.0 us)
Async XLA Ops:
  6.5 2.2 copy-start
  6.5 51.1 %all-gather.7.cloned.1.call-start = ((), (), s32[]{:S(2)}) async-start(), calls=%async_computation.1 | async-start | bytes 2621440 | tf_op jit(solution)/shard_map/all_gather | solution.py:29
  7.3 85.1 %all-gather.5.cloned.1.call-start = ((), (), s32[]{:S(2)}) async-start(), calls=%async_computation | async-start | bytes 5242880 | tf_op jit(solution)/shard_map/all_gather | solution.py:21
  8.0 237.1 %all-gather.9.cloned.1.call-start = ((), (), s32[]{:S(2)}) async-start(), calls=%async_computation.2 | async-start | bytes 10485760 | tf_op jit(solution)/shard_map/all_gather | solution.py:24
  13.9 83.2 %collective-permute-start.1 = (s32[512]{0:T(512)S(1)}, s32[512]{0:T(512)S(1)}, u32[]{:S(2)}, u32[]{:S(2)}) collective-permute-start(s32[512]{0:T(512)S(1)} %bitcast.54), channel_id=1, source_target_pairs={{0,8},{8,16},{16,24},{1,9},{9,17},{17,25},{2,10},{10,18},{18,26},{... | collective-permute-start | bytes 6152 | tf_op jit(solution)/shard_map/ppermute | solution.py:15
  96.8 1.3 collective-permute-start
  104.5 148.1 %collective-permute-start.2 = (bf16[512,256]{0,1:T(8,128)(2,1)S(1)}, bf16[512,256]{0,1:T(8,128)(2,1)S(1)}, u32[]{:S(2)}, u32[]{:S(2)}) collective-permute-start(bf16[512,256]{0,1:T(8,128)(2,1)S(1)} %all_gather.17), channel_id=1, source_target_pairs={{0,8},{8,16},{16,24},{1,9},{9,17},{17,25},{2,10},{10,18},{18,26},{... | collective-permute-start | bytes 786440 | tf_op jit(solution)/shard_map/ppermute | solution.py:15
Sparse Core Ops, SparseCore 0:
  8.9 48.6 all-gather.6
  59.2 33.1 all-gather.4
  94.0 151.0 all-gather.8
where the time goes:
time: 263 us; the launch traced here: 262 us
  waiting for transfers between devices  214 us (81%)
  matrix products  13.6 us (5%)
  between operations  13.2 us (5%)
  blocking collectives  11.5 us (4%)
  starting transfers between devices  7.78 us (3%)
    all_gather x1, waiting for transfers between devices, local(): lax.all_gather(w_query, 'ctx', axis=0, tiled=True)  137 us
    all_gather x1, waiting for transfers between devices, local(): lax.all_gather(key_value_weight, 'ctx', axis=0, tiled=True)  39.6 us
    all_gather x1, waiting for transfers between devices, local(): whole = lax.all_gather(tokens, 'col', axis=1, tiled=True)  34.8 us
    ppermute x2, starting transfers between devices, passed_along(): return lax.ppermute(x, axis, pairs)  7.39 us
    dot_general x1, matrix products, local(): jnp.dot(whole, lax.all_gather(w_query, 'ctx', axis=0, tiled=True), prefer...  6.98 us
    all_gather x1, blocking collectives, local(): lax.all_gather(joined, 'row', axis=0, tiled=True)  6.33 us
  transfers between devices with their start and end apart: 6, of which 4 were waited for; matrix products, arithmetic and copies ran while one was open for 5% of the time, Pallas kernels for 0%

commit v1 on v0

--- a/solution.py
+++ b/solution.py
@@ -18,7 +18,12 @@
 def local(tokens, w_query, key_value_weight, segment):
     half = tokens.shape[0]
     head_size = key_value_weight.shape[1]
-    whole = lax.all_gather(tokens, "col", axis=1, tiled=True)
+    ring = [tokens]
+    for hop in range(3):
+        ring.append(lax.ppermute(ring[-1], "col", [(dev, (dev + 1) % 4) for dev in range(4)]))
+    whole = jnp.roll(
+        jnp.concatenate(ring[::-1], axis=1), (lax.axis_index("col") + 1) * ring[0].shape[1], axis=1
+    )
     query_acc = jnp.dot(
         whole,
         lax.all_gather(w_query, "ctx", axis=0, tiled=True),

time: 263 us -> 227 us (0.86)
  waiting for transfers between devices: 214 us -> 167 us
  local copies, waits for them, and re-layouts: 0.85 us -> 11.7 us
    all_gather x1, waiting for transfers between devices: 39.6 us -> 0.01 us  [local(): lax.all_gather(key_value_weight, 'ctx', axis=0, tiled=True)]
    all_gather x1 -> x0, waiting for transfers between devices: 34.8 us -> none  [local(): whole = lax.all_gather(tokens, 'col', axis=1, tiled=True)]
    ppermute x0 -> x3, waiting for transfers between devices: none -> 34.4 us  [local(): lax.ppermute(ring[-1], 'col', [(dev, (dev + 1) % 4) for dev in range(4)])]
    unnamed x2 -> x11, local copies, waits for them, and re-layouts: 0.01 us -> 9.75 us
    all_gather x1, waiting for transfers between devices: 137 us -> 130 us  [local(): lax.all_gather(w_query, 'ctx', axis=0, tiled=True)]
  transfers between devices with their start and end apart: 6 -> 8, of which waited for: 4 -> 5; matrix products, arithmetic and copies ran while one was open for 5% -> 10% of each run, Pallas kernels for 0% -> 0%
where the time goes in v1:
time: 227 us
  waiting for transfers between devices  167 us (74%)
  matrix products  13.9 us (6%)
  between operations  13.6 us (6%)
  local copies, waits for them, and re-layouts  11.7 us (5%)
  blocking collectives  11.5 us (5%)
  starting transfers between devices  8.36 us (4%)
    all_gather x1, waiting for transfers between devices, local(): lax.all_gather(w_query, 'ctx', axis=0, tiled=True)  130 us
    ppermute x3, waiting for transfers between devices, local(): lax.ppermute(ring[-1], 'col', [(dev, (dev + 1) % 4) for dev in range(4)])  34.4 us
    unnamed x11, local copies, waits for them, and re-layouts  9.75 us
    ppermute x2, starting transfers between devices, passed_along(): return lax.ppermute(x, axis, pairs)  7.74 us
    all_gather x1, blocking collectives, local(): lax.all_gather(joined, 'row', axis=0, tiled=True)  7.01 us
    dot_general x1, matrix products, local(): jnp.dot(whole, lax.all_gather(w_query, 'ctx', axis=0, tiled=True), prefer...  6.98 us
    dot_general x1, matrix products, local(): jnp.dot(whole, lax.all_gather(key_value_weight, 'ctx', axis=0, tiled=True...  4.75 us
  transfers between devices with their start and end apart: 8, of which 5 were waited for; matrix products, arithmetic and copies ran while one was open for 10% of the time, Pallas kernels for 0%

profile of v1, /device:TPU:0, one launch (start us, length us, event | category | flops | bytes accessed | tf_op | source)
XLA Modules:
  0.0 226.6 jit_solution(9131993029224605362)
XLA Ops:
  6.5 0.7 all-gather.4.cloned.1.call-update
  7.3 0.7 all-gather.6.cloned.1.call-update
  8.5 14.4 %collective-permute-done = bf16[256,2048]{1,0:T(8,128)(2,1)S(1)} collective-permute-done((bf16[256,2048]{1,0:T(8,128)(2,1)S(1)}, bf16[256,2048]{1,0:T(8,128)(2,1)S(1)}, u32[]{:S(2)}, u32[]{:S(2)}) %collective-permute-start) | collective-permute-done | bytes 1048608 | tf_op jit(solution)/shard_map/ppermute | solution.py:23
  22.9 14.2 %collective-permute-done.1 = bf16[256,2048]{1,0:T(8,128)(2,1)S(1)} collective-permute-done((bf16[256,2048]{1,0:T(8,128)(2,1)S(1)}, bf16[256,2048]{1,0:T(8,128)(2,1)S(1)}, u32[]{:S(2)}, u32[]{:S(2)}) %collective-permute-start.1) | collective-permute-done | bytes 1048608 | tf_op jit(solution)/shard_map/ppermute | solution.py:23
  37.2 4.5 %all-gather = s32[2,1,256]{2,1,0:T(1,128)S(1)} all-gather(s32[1,1,256]{2,1,0:T(1,128)S(1)} %bitcast.54), channel_id=1, replica_groups=mesh['ctx'=4,'row'=2,'col'=4] {'row'}, dimensions={0}, use_global_device_ids=true | all-gather | bytes 3072 | tf_op jit(solution)/shard_map/all_gather | solution.py:46
  41.7 4.0 %collective-permute-start.4 = (s32[512]{0:T(512)S(1)}, s32[512]{0:T(512)S(1)}, u32[]{:S(2)}, u32[]{:S(2)}) collective-permute-start(s32[512]{0:T(512)S(1)} %bitcast.52), channel_id=1, source_target_pairs={{0,8},{8,16},{16,24},{1,9},{9,17},{17,25},{2,10},{10,18},{18,26},{... | collective-permute-start | bytes 6152 | tf_op jit(solution)/shard_map/ppermute | solution.py:15
  45.7 5.8 %collective-permute-done.2 = bf16[256,2048]{1,0:T(8,128)(2,1)} collective-permute-done((bf16[256,2048]{1,0:T(8,128)(2,1)S(1)}, bf16[256,2048]{1,0:T(8,128)(2,1)}, u32[]{:S(2)}, u32[]{:S(2)}) %collective-permute-start.2) | collective-permute-done | bytes 1048608 | tf_op jit(solution)/shard_map/ppermute | solution.py:23
  51.5 2.3 %constant_dynamic-update-slice_fusion.7 = bf16[256,16384]{1,0:T(8,128)(2,1)} fusion(bf16[256,2048]{1,0:T(8,128)(2,1)} %collective-permute-done.2), kind=kLoop, calls=%fused_computation.48 | loop fusion | bytes 2097152
  53.8 1.0 constant_dynamic-update-slice_fusion.6
  54.8 1.0 constant_dynamic-update-slice_fusion.5
  55.8 1.1 constant_dynamic-update-slice_fusion.4
  56.9 2.3 %constant_dynamic-update-slice_fusion.3 = bf16[256,16384]{1,0:T(8,128)(2,1)} fusion(bf16[256,16384]{1,0:T(8,128)(2,1)} %constant_dynamic-update-slice_fusion.4, bf16[256,2048]{1,0:T(8,128)(2,1)} %collective-permute-done.2), kind=kLoop, calls=%fused_computation.44 | loop fusion | bytes 2097152
  59.2 1.0 constant_dynamic-update-slice_fusion.2
  60.2 1.0 constant_dynamic-update-slice_fusion.1
  61.2 1.1 constant_dynamic-update-slice_fusion
  62.3 4.7 %fusion.18 = bf16[256,128]{0,1:T(8,128)(2,1)S(1)} fusion(bf16[8192,128]{1,0:T(8,128)(2,1)} %all-gather.4.cloned.1.call-done, bf16[256,16384]{1,0:T(8,128)(2,1)} %constant_dynamic-update-slice_fusion, s32[]{:T(128)S(6)} %select_n.41), kind=kOutput, calls=%fused_computation.19 | convolution fusion | flops 536903680 | bytes 6356996 | tf_op jit(solution)/shard_map/dot_general | solution.py:32
  67.4 1.0 collective-permute-done.3
  68.4 7.0 %all_gather.13 = bf16[512,256]{0,1:T(8,128)(2,1)S(1)} all-gather(bf16[256,256]{0,1:T(8,128)(2,1)S(1)} %pad_maximum_fusion), channel_id=1, replica_groups=mesh['ctx'=4,'row'=2,'col'=4] {'row'}, dimensions={0}, use_global_device_ids=true | all-gather | bytes 393216 | tf_op jit(solution)/shard_map/all_gather | solution.py:45
  75.4 3.7 %collective-permute-start.5 = (bf16[512,256]{0,1:T(8,128)(2,1)S(1)}, bf16[512,256]{0,1:T(8,128)(2,1)S(1)}, u32[]{:S(2)}, u32[]{:S(2)}) collective-permute-start(bf16[512,256]{0,1:T(8,128)(2,1)S(1)} %all_gather.13), channel_id=1, source_target_pairs={{0,8},{8,16},{16,24},{1,9},{9,17},{17,25},{2,10},{10,18},{18,26},{... | collective-permute-start | bytes 786440 | tf_op jit(solution)/shard_map/ppermute | solution.py:15
  79.2 129.8 %all-gather.6.cloned.1.call-done = bf16[8192,512]{1,0:T(8,128)(2,1)} async-done(((bf16[2048,512]{1,0:T(8,128)(2,1)}), bf16[8192,512]{1,0:T(8,128)(2,1)}) %all-gather.6.cloned.1.call-update) | async-done | bytes 8388624 | tf_op jit(solution)/shard_map/all_gather | solution.py:29
  209.0 7.0 %fusion.15 = bf16[32,4,8,128]{3,2,1,0:T(8,128)(2,1)S(1)} fusion(bf16[8192,512]{1,0:T(8,128)(2,1)} %all-gather.6.cloned.1.call-done, bf16[256,16384]{1,0:T(8,128)(2,1)} %constant_dynamic-update-slice_fusion, s32[]{:T(128)S(6)} %select_n.41), kind=kOutput, calls=%fused_computation.18 | convolution fusion | flops 2147614720 | bytes 12845060 | tf_op jit(solution)/shard_map/dot_general | solution.py:27
  217.5 0.7 fusion.6
  218.2 0.7 fusion.11
  219.0 0.8 copy.18
  (22 shorter events, 2.4 us)
Async XLA Ops:
  6.5 1.5 copy-start
  6.5 30.6 %copy-start.1 = (s32[256]{0:T(256)S(1)}, s32[256]{0:T(256)}, u32[]{:S(2)}) copy-start(s32[256]{0:T(256)} %param.7) | copy-start | bytes 3076
  6.5 55.8 %all-gather.4.cloned.1.call-start = ((), (), s32[]{:S(2)}) async-start(), calls=%async_computation | async-start | bytes 2621440 | tf_op jit(solution)/shard_map/all_gather | solution.py:34
  7.3 201.7 %all-gather.6.cloned.1.call-start = ((), (), s32[]{:S(2)}) async-start(), calls=%async_computation.1 | async-start | bytes 10485760 | tf_op jit(solution)/shard_map/all_gather | solution.py:29
  8.0 14.9 %collective-permute-start = (bf16[256,2048]{1,0:T(8,128)(2,1)S(1)}, bf16[256,2048]{1,0:T(8,128)(2,1)S(1)}, u32[]{:S(2)}, u32[]{:S(2)}) collective-permute-start(bf16[256,2048]{1,0:T(8,128)(2,1)S(1)} %copy-done), channel_id=1, source_target_pairs={{0,1},{1,2},{2,3},{3,0},{4,5},{5,6},{6,7},{7,4},{8,9},{9,10},{10,1... | collective-permute-start | bytes 3145736 | tf_op jit(solution)/shard_map/ppermute | solution.py:23
  22.9 14.2 %collective-permute-start.1 = (bf16[256,2048]{1,0:T(8,128)(2,1)S(1)}, bf16[256,2048]{1,0:T(8,128)(2,1)S(1)}, u32[]{:S(2)}, u32[]{:S(2)}) collective-permute-start(bf16[256,2048]{1,0:T(8,128)(2,1)S(1)} %collective-permute-done), channel_id=1, source_target_pairs={{0,1},{1,2},{2,3},{3,0},{4,5},{5,6},{6,7},{7,4},{8,9},{9,10},{10,1... | collective-permute-start | bytes 3145736 | tf_op jit(solution)/shard_map/ppermute | solution.py:23
  37.2 14.3 %collective-permute-start.2 = (bf16[256,2048]{1,0:T(8,128)(2,1)S(1)}, bf16[256,2048]{1,0:T(8,128)(2,1)}, u32[]{:S(2)}, u32[]{:S(2)}) collective-permute-start(bf16[256,2048]{1,0:T(8,128)(2,1)S(1)} %collective-permute-done.1), channel_id=1, source_target_pairs={{0,1},{1,2},{2,3},{3,0},{4,5},{5,6},{6,7},{7,4},{8,9},{9,10},{10,1... | collective-permute-start | bytes 3145736 | tf_op jit(solution)/shard_map/ppermute | solution.py:23
  41.7 25.5 %collective-permute-start.4 = (s32[512]{0:T(512)S(1)}, s32[512]{0:T(512)S(1)}, u32[]{:S(2)}, u32[]{:S(2)}) collective-permute-start(s32[512]{0:T(512)S(1)} %bitcast.52), channel_id=1, source_target_pairs={{0,8},{8,16},{16,24},{1,9},{9,17},{17,25},{2,10},{10,18},{18,26},{... | collective-permute-start | bytes 6152 | tf_op jit(solution)/shard_map/ppermute | solution.py:15
  67.1 1.3 collective-permute-start.3
  75.4 141.0 %collective-permute-start.5 = (bf16[512,256]{0,1:T(8,128)(2,1)S(1)}, bf16[512,256]{0,1:T(8,128)(2,1)S(1)}, u32[]{:S(2)}, u32[]{:S(2)}) collective-permute-start(bf16[512,256]{0,1:T(8,128)(2,1)S(1)} %all_gather.13), channel_id=1, source_target_pairs={{0,8},{8,16},{16,24},{1,9},{9,17},{17,25},{2,10},{10,18},{18,26},{... | collective-permute-start | bytes 786440 | tf_op jit(solution)/shard_map/ppermute | solution.py:15
Sparse Core Ops, SparseCore 0:
  8.9 48.6 all-gather.3
  59.2 149.7 all-gather.5
